TPU v7x, 256 devices: a whole 4x4x8 slice. The times are simulated.
256 devices in a mesh: grp: 8 (over y, core), seq: 32 (over z, x).
Axes of the slice: x: 4, y: 4, z: 8, core: 2. Of those that a mesh axis runs over, the one named last changes fastest.
Arguments:
- query_rows: bfloat16 [1, 32768, 1024], P(None, ('grp', 'seq')), may hold values from -6 to 6
- key_rows: bfloat16 [1, 32768, 1024], P(None, ('grp', 'seq')), may hold values from -6 to 6
- value_rows: bfloat16 [1, 32768, 1024], P(None, ('grp', 'seq')), may hold values from -6 to 6
- teacher: bfloat16 [1, 32768, 1024], P(None, ('grp', 'seq')), may hold values from -4 to 4
- query_map: bfloat16 [8, 128, 64], replicated, may hold values from -0.5 to 0.5
- key_map: bfloat16 [8, 128, 64], replicated, may hold values from -0.5 to 0.5
- decay_rate: float32 [1, 8, 32768], P(None, None, ('grp', 'seq')), may hold values from 0 to 1, as said below
Outputs:
- mismatch: float32 [1, 32768, 1024], P(None, ('grp', 'seq'))
Inputs may be any that keep to these rules, and one draw needn't show every extreme that they name: `decay_rate`: rates are non-negative; a state is multiplied by exp(-rate) at each position.
All inputs are finite; a program needn't handle non-finite values.
Results may differ from a plain program's by a relative error of at most 0.00037.
Values sent between devices are 32-bit elements; how exact they have to be, the bound alone decides.
A program may use at most 256 MiB of HBM per device.

v0:
```python
import functools

import jax
import jax.numpy as jnp
from jax import lax
from jax.experimental import pallas as pl
from jax.experimental.pallas import tpu as pltpu
from jax.sharding import PartitionSpec as P

MESH = pl.DeviceIdType.MESH
F32 = jnp.float32
BF16 = jnp.bfloat16

NX, NZ, NG = 4, 8, 8
HEADS = 8
T = 128
SLICE = HEADS * T // (NX * NZ)
PER_HEAD = T // SLICE


def softplus(p):
    return jnp.maximum(p, 0.0) + jnp.log1p(jnp.exp(-jnp.abs(p)))


def dot(a, b, dims=((1,), (0,))):
    return lax.dot_general(a, b, (dims, ((), ())), preferred_element_type=F32)


def kernel(
    q_ref, k_ref, v_ref, t_ref, wq_ref, wk_ref, rate_ref, o_ref,
    own, xin, tout, zin, gin, wout, cin, vout, fin,
    auxx, auxz, auxg, phiq, phik, run_col, den,
    s_ax, r_ax, s_az, r_az, s_ag, r_ag,
    s_x, r_x, s_z, r_z, s_g, r_g, s_w, r_w, s_v, r_v,
):
    g = lax.axis_index("grp")
    s = lax.axis_index("seq")
    z, x = s // NX, s % NX

    def at_x(i):
        return (g, z * NX + i)

    def at_z(i):
        return (g, i * NX + x)

    def at_g(i):
        return (i, s)

    def copy(src, dst, ssem, rsem, to):
        return pltpu.make_async_remote_copy(
            src_ref=src, dst_ref=dst, send_sem=ssem, recv_sem=rsem, device_id=to, device_id_type=MESH
        )

    other_x = [(x + d) % NX for d in (2, 1, 3)]
    other_z = [(z + d) % NZ for d in (4, 3, 5, 2, 6, 1, 7)]
    other_g = [(g + d) % NG for d in (4, 3, 5, 2, 6, 1, 7)]

    barrier = pltpu.get_barrier_semaphore()
    for to in [at_x(i) for i in other_x] + [at_z(i) for i in other_z] + [at_g(i) for i in other_g]:
        pl.semaphore_signal(barrier, inc=1, device_id=to, device_id_type=MESH)

    lane = lax.broadcasted_iota(jnp.int32, (HEADS, T), 1)
    running = rate_ref[...]
    step = 1
    while step < T:
        running = running + jnp.where(lane >= step, pltpu.roll(running, step, 1), 0.0)
        step *= 2
    total = jnp.broadcast_to(running[:, T - 1 : T], (HEADS, T))
    columns = running.T
    fade = jnp.exp(-(total - running)).T
    run_col[...] = columns

    for h in range(HEADS):
        at = pl.ds(h * T, T)
        w = wk_ref[h]
        phi = softplus(dot(k_ref[:, at], jnp.concatenate([w, -w], axis=-1))).astype(BF16)
        phik[h] = phi
        faded = phi.astype(F32) * fade[:, h : h + 1]
        auxx[x, pl.ds(h, 1), :] = jnp.sum(faded, axis=0, keepdims=True)
        own[at, :] = dot(faded.astype(BF16), v_ref[:, at], ((0,), (0,)))
    auxx[x, pl.ds(HEADS, HEADS), :] = jnp.exp(-total)
    quarter = HEADS * T // NX
    xin[x] = own[pl.ds(pl.multiple_of(x * quarter, quarter), quarter), :].reshape(NZ, SLICE, T)

    pl.semaphore_wait(barrier, len(other_x) + len(other_z) + len(other_g))

    sent = []

    def send(*args):
        c = copy(*args)
        c.start()
        sent.append(c)

    for n, i in enumerate(other_x):
        send(auxx.at[x], auxx.at[x], s_ax.at[n], r_ax.at[x], at_x(i))
    order = other_z + [z]
    for m, c in enumerate(order):
        for n, i in enumerate(other_x):
            row = pl.multiple_of(i * quarter + c * SLICE, SLICE)
            send(own.at[pl.ds(row, SLICE)], xin.at[x, c], s_x.at[n * NZ + m], r_x.at[x * NZ + c], at_x(i))

    causal = lax.broadcasted_iota(jnp.int32, (T, T), 0) >= lax.broadcasted_iota(jnp.int32, (T, T), 1)

    def attend(h):
        at = pl.ds(h * T, T)
        w = wq_ref[h]
        phi = softplus(dot(q_ref[:, at], jnp.concatenate([w, -w], axis=-1))).astype(BF16)
        phiq[h] = phi
        scores = dot(phi, phik[h], ((1,), (1,)))
        spacing = columns[:, h : h + 1] - running[h : h + 1, :]
        weighted = jnp.where(causal, scores * jnp.exp(-spacing), 0.0)
        den[:, h : h + 1] = jnp.sum(weighted, axis=1, keepdims=True)
        o_ref[:, at] = dot(weighted.astype(BF16), v_ref[:, at])

    for h in range(0, 2):
        attend(h)

    for i in other_x:
        copy(auxx.at[x], auxx.at[i], s_ax.at[0], r_ax.at[i], at_x(i)).wait_recv()
    zero = jnp.zeros((HEADS, T), F32)
    one = jnp.ones((HEADS, T), F32)

    def chain(aux, n, here):
        norm, decay, norm_before, decay_before = zero, one, zero, one
        for i in range(n):
            norm_before = jnp.where(here == i, norm, norm_before)
            decay_before = jnp.where(here == i, decay, decay_before)
            d = aux[i, pl.ds(HEADS, HEADS), :]
            norm = d * norm + aux[i, pl.ds(0, HEADS), :]
            decay = d * decay
        return norm, decay, norm_before, decay_before

    norm, decay, norm_x, decay_x = chain(auxx, NX, x)
    auxz[z, pl.ds(0, HEADS), :] = norm
    auxz[z, pl.ds(HEADS, HEADS), :] = decay
    for n, i in enumerate(other_z):
        send(auxz.at[z], auxz.at[z], s_az.at[n], r_az.at[z], at_z(i))

    def head_row(aux, i, c):
        head = (x * NZ + c) // PER_HEAD
        return aux[i, pl.ds(HEADS + head, 1), :]

    for n, c in enumerate(order):
        for i in other_x:
            copy(own.at[pl.ds(0, SLICE)], xin.at[i, c], s_x.at[0], r_x.at[i * NZ + c], at_x(i)).wait_recv()
        acc = xin[0, c]
        for i in range(1, NX):
            acc = head_row(auxx, i, c) * acc + xin[i, c]
        if n < NZ - 1:
            tout[n] = acc
            send(tout.at[n], zin.at[z], s_z.at[n], r_z.at[z], at_z(c))
        else:
            zin[z] = acc

    for h in range(2, 5):
        attend(h)

    for i in other_z:
        copy(auxz.at[z], auxz.at[i], s_az.at[0], r_az.at[i], at_z(i)).wait_recv()
    norm, decay, norm_z, decay_z = chain(auxz, NZ, z)
    auxg[g, pl.ds(0, HEADS), :] = norm
    auxg[g, pl.ds(HEADS, HEADS), :] = decay
    for n, i in enumerate(other_g):
        send(auxg.at[g], auxg.at[g], s_ag.at[n], r_ag.at[g], at_g(i))
    for i in other_z:
        copy(tout.at[0], zin.at[i], s_z.at[0], r_z.at[i], at_z(i)).wait_recv()
    acc = zin[0]
    for i in range(1, NZ):
        acc = head_row(auxz, i, z) * acc + zin[i]
    gin[g] = acc
    for n, i in enumerate(other_g):
        send(gin.at[g], gin.at[g], s_g.at[n], r_g.at[g], at_g(i))

    for h in range(5, 8):
        attend(h)

    for i in other_g:
        copy(auxg.at[g], auxg.at[i], s_ag.at[0], r_ag.at[i], at_g(i)).wait_recv()
    for i in other_g:
        copy(gin.at[g], gin.at[i], s_g.at[0], r_g.at[i], at_g(i)).wait_recv()
    acc = jnp.zeros((SLICE, T), F32)
    for i in range(NG - 1):
        acc = jnp.where(i < g, head_row(auxg, i, z) * acc + gin[i], acc)
    for i in range(NZ):
        wout[i] = acc
        if i < NZ - 1:
            acc = head_row(auxz, i, z) * acc + zin[i]
    cin[z] = wout[z]
    for n, i in enumerate(other_z):
        send(wout.at[i], cin.at[z], s_w.at[n], r_w.at[z], at_z(i))

    _, _, norm_g, _ = chain(auxg, NG, g)
    norm_in = decay_x * (decay_z * norm_g + norm_z) + norm_x
    lead = jnp.exp(-columns)
    for h in range(HEADS):
        at = pl.ds(h * T, T)
        from_norm = jnp.sum(phiq[h].astype(F32) * norm_in[h : h + 1, :], axis=1, keepdims=True)
        inverse = 1.0 / (den[:, h : h + 1] + lead[:, h : h + 1] * from_norm)
        o_ref[:, at] = o_ref[:, at] * inverse - t_ref[:, at].astype(F32)
        den[:, h : h + 1] = lead[:, h : h + 1] * inverse

    for m, c in enumerate([z] + other_z[::-1]):
        if m:
            copy(wout.at[0], cin.at[c], s_w.at[0], r_w.at[c], at_z(c)).wait_recv()
        acc = cin[c]
        for i in range(NX):
            vout[i, c] = acc
            if i < NX - 1:
                acc = head_row(auxx, i, c) * acc + xin[i, c]
        for n, i in enumerate(other_x):
            send(vout.at[i, c], fin.at[x, c], s_v.at[n * NZ + m], r_v.at[x * NZ + c], at_x(i))
    fin[x] = vout[x]

    per_x = HEADS // NX
    for h in range(HEADS):
        at = pl.ds(h * T, T)
        owner, first = h // per_x, (h % per_x) * PER_HEAD

        @pl.when(owner != x)
        def _():
            for c in range(first, first + PER_HEAD):
                copy(vout.at[0, 0], fin.at[owner, c], s_v.at[0], r_v.at[owner * NZ + c], at_x(owner)).wait_recv()

        state = fin[owner, pl.ds(first, PER_HEAD)].reshape(T, T)
        high = state.astype(BF16)
        low = (state - high.astype(F32)).astype(BF16)
        phi = phiq[h]
        o_ref[:, at] = o_ref[:, at] + den[:, h : h + 1] * (dot(phi, high) + dot(phi, low))

    for c in sent:
        c.wait_send()


def local(query_rows, key_rows, value_rows, teacher, query_map, key_map, decay_rate):
    shape = query_rows.shape[1:]
    vmem = pl.BlockSpec(memory_space=pltpu.VMEM)
    dma = lambda n: pltpu.SemaphoreType.DMA((n,))
    part = lambda *lead: pltpu.VMEM(lead + (SLICE, T), F32)
    aux = lambda n: pltpu.VMEM((n, 2 * HEADS, T), F32)
    out = pl.pallas_call(
        kernel,
        out_shape=jax.ShapeDtypeStruct(shape, F32),
        in_specs=[vmem] * 7,
        out_specs=vmem,
        scratch_shapes=[
            pltpu.VMEM((HEADS * T, T), F32),
            part(NX, NZ),
            part(NZ - 1),
            part(NZ),
            part(NG),
            part(NZ),
            part(NZ),
            part(NX, NZ),
            part(NX, NZ),
            aux(NX),
            aux(NZ),
            aux(NG),
            pltpu.VMEM((HEADS, T, T), BF16),
            pltpu.VMEM((HEADS, T, T), BF16),
            pltpu.VMEM((T, HEADS), F32),
            pltpu.VMEM((T, HEADS), F32),
            dma(NX - 1), dma(NX), dma(NZ - 1), dma(NZ), dma(NG - 1), dma(NG),
            dma((NX - 1) * NZ), dma(NX * NZ), dma(NZ - 1), dma(NZ), dma(NG - 1), dma(NG),
            dma(NZ - 1), dma(NZ), dma((NX - 1) * NZ), dma(NX * NZ),
        ],
        compiler_params=pltpu.CompilerParams(
            collective_id=0, has_side_effects=True, vmem_limit_bytes=32 * 1024 * 1024
        ),
    )(
        query_rows.reshape(shape),
        key_rows.reshape(shape),
        value_rows.reshape(shape),
        teacher.reshape(shape),
        query_map,
        key_map,
        decay_rate.reshape(decay_rate.shape[1:]),
    )
    return out.reshape(query_rows.shape)


def solution(mesh):
    rows = P(None, ("grp", "seq"), None)
    return jax.shard_map(
        local,
        mesh=mesh,
        in_specs=(rows, rows, rows, rows, P(), P(), P(None, None, ("grp", "seq"))),
        out_specs=rows,
        check_vma=False,
    )
```

profile of v0, /device:TPU:1, one launch (start us, length us, event | category | flops | bytes accessed | tf_op | source)
XLA Modules:
  0.0 43.2 jit_solution(5864894235185809865)
XLA Ops:
  0.0 0.0 copy-start.4
  0.0 0.0 copy-start.1
  0.0 0.0 copy-start.2
  0.0 1.1 %copy.8.wq_ref = bf16[8,128,64]{2,1,0:T(8,128)(2,1)S(1)} copy(bf16[8,128,64]{1,2,0:T(8,128)(2,1)} %param.11) | data formatting | bytes 262144 | tf_op args[4]
  1.1 0.0 copy-start
  1.2 1.1 %copy.9.wk_ref = bf16[8,128,64]{2,1,0:T(8,128)(2,1)S(1)} copy(bf16[8,128,64]{1,2,0:T(8,128)(2,1)} %param.12) | data formatting | bytes 262144 | tf_op args[5]
  2.3 0.0 copy-done.4
  2.3 0.0 copy-done.1
  2.3 0.0 copy-done.2
  2.3 0.0 copy-done
  2.3 0.0 copy-start.3
  2.3 0.9 %copy-done.3 = bf16[1,128,1024]{2,1,0:T(8,128)(2,1)S(1)} copy-done((bf16[1,128,1024]{2,1,0:T(8,128)(2,1)S(1)}, bf16[1,128,1024]{2,1,0:T(8,128)(2,1)}, u32[]{:S(2)}) %copy-start.3) | copy-done | bytes 262168
  3.3 39.2 %shard_map.73 = f32[128,1024]{1,0:T(8,128)S(1)} custom-call(bf16[128,1024]{1,0:T(8,128)(2,1)S(1)} %bitcast.7, bf16[128,1024]{1,0:T(8,128)(2,1)S(1)} %bitcast.8, bf16[128,1024]{1,0:T(8,128)(2,1)S(1)} %bitcast.9, bf16[128,1024]{1,0:T(8,128)(2,1)S(1)} %bitcast.10, bf16[8,128,64]{2,1,0:T(8,128)(2,1)S(1)} %copy.8.wq_ref, bf16[8,128,64]{2,1,0:T(8,128)(2,1)S(1)} %copy.9.wk_ref, ...), custom_call_target="tpu_custom_call" | custom-call | tf_op jit(solution)/shard_map/pallas_call | solution.py:240
  42.4 0.8 %copy.11 = f32[1,128,1024]{2,1,0:T(8,128)} copy(f32[1,128,1024]{2,1,0:T(8,128)S(1)} %bitcast.6) | data formatting | bytes 1048576
Async XLA Ops:
  0.0 2.3 %copy-start.4 = (f32[1,8,128]{2,1,0:T(8,128)S(1)}, f32[1,8,128]{2,1,0:T(8,128)}, u32[]{:S(2)}) copy-start(f32[1,8,128]{2,1,0:T(8,128)} %param.13) | copy-start | bytes 12292
  0.0 2.3 %copy-start.1 = (bf16[1,128,1024]{2,1,0:T(8,128)(2,1)S(1)}, bf16[1,128,1024]{2,1,0:T(8,128)(2,1)}, u32[]{:S(2)}) copy-start(bf16[1,128,1024]{2,1,0:T(8,128)(2,1)} %param.8) | copy-start | bytes 786436
  0.0 2.3 %copy-start.2 = (bf16[1,128,1024]{2,1,0:T(8,128)(2,1)S(1)}, bf16[1,128,1024]{2,1,0:T(8,128)(2,1)}, u32[]{:S(2)}) copy-start(bf16[1,128,1024]{2,1,0:T(8,128)(2,1)} %param.9) | copy-start | bytes 786436
  1.1 1.2 %copy-start = (bf16[1,128,1024]{2,1,0:T(8,128)(2,1)S(1)}, bf16[1,128,1024]{2,1,0:T(8,128)(2,1)}, u32[]{:S(2)}) copy-start(bf16[1,128,1024]{2,1,0:T(8,128)(2,1)} %param.7) | copy-start | bytes 786436
  2.3 1.0 %copy-start.3 = (bf16[1,128,1024]{2,1,0:T(8,128)(2,1)S(1)}, bf16[1,128,1024]{2,1,0:T(8,128)(2,1)}, u32[]{:S(2)}) copy-start(bf16[1,128,1024]{2,1,0:T(8,128)(2,1)} %param.10) | copy-start | bytes 786436
where the time goes:
time: 43.4 us; the launch traced here: 43.2 us
  Pallas kernels  39.2 us (90%)
  local copies, waits for them, and re-layouts  4.01 us (9%)
    pallas_call x1, Pallas kernels, local(): pl.pallas_call(kernel, out_shape=jax.ShapeDtypeStruct(shape, F32), in_spe...  39.2 us
    unnamed x13, local copies, waits for them, and re-layouts  4.01 us

commit v1 on v0

v1 whole, which is shorter than its diff:
```python
import jax
import jax.numpy as jnp
from jax import lax
from jax.experimental import pallas as pl
from jax.experimental.pallas import tpu as pltpu
from jax.sharding import PartitionSpec as P

MESH = pl.DeviceIdType.MESH
F32 = jnp.float32
BF16 = jnp.bfloat16

NX, NZ, NG = 4, 8, 8
HEADS = 8
T = 128
SLICE = HEADS * T // (NX * NZ)
PER_HEAD = T // SLICE
PER_X = HEADS // NX
ROW = pl.ds(0, HEADS)
DECAY = pl.ds(HEADS, HEADS)


def dot(a, b, dims=((1,), (0,))):
    return lax.dot_general(a, b, (dims, ((), ())), preferred_element_type=F32)


def lanes(h):
    return pl.ds(h * T, T) if isinstance(h, int) else pl.ds(pl.multiple_of(h * T, T), T)


def kernel(
    q_hbm, k_hbm, v_hbm, t_hbm, wq_hbm, wk_hbm, rate_hbm, o_ref,
    q_ref, k_ref, v_ref, t_ref, wq_ref, wk_ref, rate_ref,
    own, xin, before, term, tout, zin, gin, wout, cin, fin,
    dx, nx, auxz, auxg, phiq, phik, run, run_col, den,
    s_in, s_dx, r_dx, s_nx, r_nx, s_az, r_az, s_ag, r_ag,
    s_x, r_x, s_z, r_z, s_g, r_g, s_w, r_w, s_v, r_v, s_t, r_t,
):
    g = lax.axis_index("grp")
    s = lax.axis_index("seq")
    z, x = s // NX, s % NX

    def at_x(i):
        return (g, z * NX + i)

    def at_z(i):
        return (g, i * NX + x)

    def at_g(i):
        return (i, s)

    def copy(src, dst, ssem, rsem, to):
        return pltpu.make_async_remote_copy(
            src_ref=src, dst_ref=dst, send_sem=ssem, recv_sem=rsem, device_id=to, device_id_type=MESH
        )

    other_x = [(x + d) % NX for d in (2, 1, 3)]
    other_z = [(z + d) % NZ for d in (4, 3, 5, 2, 6, 1, 7)]
    order = other_z + [z]
    other_g = [(g + d) % NG for d in (4, 3, 5, 2, 6, 1, 7)]

    barrier = pltpu.get_barrier_semaphore()
    for to in [at_z(i) for i in other_z] + [at_g(i) for i in other_g] + [at_x(i) for i in other_x]:
        pl.semaphore_signal(barrier, inc=1, device_id=to, device_id_type=MESH)

    pairs = [
        (rate_hbm, rate_ref), (wk_hbm, wk_ref), (k_hbm, k_ref), (v_hbm, v_ref),
        (wq_hbm, wq_ref), (q_hbm, q_ref), (t_hbm, t_ref),
    ]
    loads = [pltpu.make_async_copy(a, b, s_in.at[n]) for n, (a, b) in enumerate(pairs)]
    for load in loads:
        load.start()

    sent = []

    def send(*args):
        c = copy(*args)
        c.start()
        sent.append(c)

    loads[0].wait()
    lane = lax.broadcasted_iota(jnp.int32, (HEADS, T), 1)
    running = rate_ref[...]
    step = 1
    while step < T:
        running = running + jnp.where(lane >= step, pltpu.roll(running, step, 1), 0.0)
        step *= 2
    total = jnp.broadcast_to(running[:, T - 1 : T], (HEADS, T))
    run[ROW, :] = running
    run[DECAY, :] = jnp.exp(running - total)
    dx[x] = jnp.exp(-total)

    half = NZ // 2

    def states(e):
        for p in range(NX):
            h = PER_X * p + e
            product = dot(wk_ref[h], k_ref[:, lanes(h)], ((1,), (1,)))
            both = jnp.log1p(jnp.exp(-jnp.abs(product)))
            phi = jnp.concatenate([jnp.maximum(product, 0.0) + both, jnp.maximum(-product, 0.0) + both], axis=0)
            phi = phi.astype(BF16)
            phik[h] = phi
            faded = phi.astype(F32) * run[pl.ds(HEADS + h, 1), :]
            own[p, pl.ds(e * half, half)] = dot(faded.astype(BF16), v_ref[:, lanes(h)]).reshape(half, SLICE, T)

    def send_slices(m0, slots):
        for m, c in enumerate(slots):
            for n, i in enumerate(other_x):
                send(own.at[i, c], xin.at[x, c], s_x.at[n * NZ + m0 + m], r_x.at[x * NZ + c], at_x(i))

    loads[1].wait()
    loads[2].wait()
    loads[3].wait()
    states(0)
    states(1)
    for h in range(HEADS):
        fade = run[pl.ds(HEADS + h, 1), :]
        high = fade.astype(BF16)
        low = (fade - high.astype(F32)).astype(BF16)
        sums = dot(jnp.concatenate([high, low], axis=0), phik[h], ((1,), (1,)))
        nx[x, pl.ds(h, 1), :] = sums[0:1, :] + sums[1:2, :]
    pl.semaphore_wait(barrier, len(other_x) + len(other_z) + len(other_g))
    for n, i in enumerate(other_x):
        send(dx.at[x], dx.at[x], s_dx.at[n], r_dx.at[x], at_x(i))
    send_slices(0, order[:half])
    for n, i in enumerate(other_x):
        send(nx.at[x], nx.at[x], s_nx.at[n], r_nx.at[x], at_x(i))
    send_slices(half, order[half:])
    xin[x] = own[x]

    causal = lax.broadcasted_iota(jnp.int32, (T, T), 0) >= lax.broadcasted_iota(jnp.int32, (T, T), 1)
    loads[4].wait()
    loads[5].wait()
    loads[6].wait()
    for h in range(HEADS):
        w = wq_ref[h]
        product = dot(q_ref[:, lanes(h)], jnp.concatenate([w, -w], axis=0), ((1,), (1,)))
        phi = (jnp.maximum(product, 0.0) + jnp.log1p(jnp.exp(-jnp.abs(product)))).astype(BF16)
        phiq[h] = phi
        column = jnp.broadcast_to(run[pl.ds(h, 1), :], (T, T)).T
        run_col[h] = column
        scores = dot(phi, phik[h])
        weighted = jnp.where(causal, scores * jnp.exp(run[pl.ds(h, 1), :] - column), 0.0)
        den[h] = jnp.broadcast_to(jnp.sum(weighted, axis=1, keepdims=True), (T, T))
        o_ref[:, lanes(h)] = dot(weighted.astype(BF16), v_ref[:, lanes(h)])

    def head_row(ref, i, c, first):
        return ref[i, pl.ds(first + (x * NZ + c) // PER_HEAD, 1), :]

    def row_totals(m0, slots):
        for m, c in enumerate(slots):
            for i in other_x:
                copy(own.at[0, 0], xin.at[i, c], s_x.at[0], r_x.at[i * NZ + c], at_x(i)).wait_recv()
            acc = jnp.zeros((SLICE, T), F32)
            for i in range(NX):
                before[i, c] = acc
                acc = head_row(dx, i, c, 0) * acc + xin[i, c]
            if m0 + m < NZ - 1:
                tout[m0 + m] = acc
                send(tout.at[m0 + m], zin.at[z], s_z.at[m0 + m], r_z.at[z], at_z(c))
            else:
                zin[z] = acc

    for i in other_x:
        copy(dx.at[x], dx.at[i], s_dx.at[0], r_dx.at[i], at_x(i)).wait_recv()
    row_totals(0, order[:half])

    def chain(parts, here):
        norm, decay = jnp.zeros((HEADS, T), F32), jnp.ones((HEADS, T), F32)
        norm_before, decay_before = norm, decay
        for i, (n, d) in enumerate(parts):
            norm_before = jnp.where(here == i, norm, norm_before)
            decay_before = jnp.where(here == i, decay, decay_before)
            norm = d * norm + n
            decay = d * decay
        return norm, decay, norm_before, decay_before

    for i in other_x:
        copy(nx.at[x], nx.at[i], s_nx.at[0], r_nx.at[i], at_x(i)).wait_recv()
    norm, decay, norm_x, decay_x = chain([(nx[i], dx[i]) for i in range(NX)], x)
    auxz[z, ROW, :] = norm
    auxz[z, DECAY, :] = decay
    for n, i in enumerate(other_z):
        send(auxz.at[z], auxz.at[z], s_az.at[n], r_az.at[z], at_z(i))
    row_totals(half, order[half:])
    for n, i in enumerate(other_x):
        send(before.at[i], term.at[x], s_t.at[n], r_t.at[x], at_x(i))

    for i in other_z:
        copy(auxz.at[z], auxz.at[i], s_az.at[0], r_az.at[i], at_z(i)).wait_recv()
    norm, decay, norm_z, decay_z = chain([(auxz[i, ROW, :], auxz[i, DECAY, :]) for i in range(NZ)], z)
    auxg[g, ROW, :] = norm
    auxg[g, DECAY, :] = decay

    def each_later(act):
        for i in range(1, NG):
            @pl.when(i > g)
            def _(i=i):
                act(i)

    def each_earlier(act):
        for i in range(NG - 1):
            @pl.when(i < g)
            def _(i=i):
                act(i)

    def aux_to(i):
        return copy(auxg.at[g], auxg.at[g], s_ag.at[i], r_ag.at[g], at_g(i))

    def total_to(i):
        return copy(gin.at[g], gin.at[g], s_g.at[i], r_g.at[g], at_g(i))

    each_later(lambda i: aux_to(i).start())
    for i in other_z:
        copy(tout.at[0], zin.at[i], s_z.at[0], r_z.at[i], at_z(i)).wait_recv()
    acc = zin[0]
    for i in range(1, NZ):
        acc = head_row(auxz, i, z, HEADS) * acc + zin[i]
    gin[g] = acc
    each_later(lambda i: total_to(i).start())

    each_earlier(lambda i: copy(auxg.at[g], auxg.at[i], s_ag.at[0], r_ag.at[i], at_g(i)).wait_recv())
    each_earlier(lambda i: copy(gin.at[g], gin.at[i], s_g.at[0], r_g.at[i], at_g(i)).wait_recv())
    acc = jnp.zeros((SLICE, T), F32)
    for i in range(NG - 1):
        acc = jnp.where(i < g, head_row(auxg, i, z, HEADS) * acc + gin[i], acc)

    def carry_to(i):
        return copy(wout.at[i], cin.at[z], s_w.at[i], r_w.at[z], at_z(i))

    for i in range(NZ):
        wout[i] = acc

        @pl.when(i != z)
        def _(i=i):
            carry_to(i).start()

        if i < NZ - 1:
            acc = head_row(auxz, i, z, HEADS) * acc + zin[i]
    cin[z] = wout[z]

    norm_g = jnp.zeros((HEADS, T), F32)
    for i in range(NG - 1):
        norm_g = jnp.where(i < g, auxg[i, DECAY, :] * norm_g + auxg[i, ROW, :], norm_g)
    norm_in = decay_x * (decay_z * norm_g + norm_z) + norm_x
    for h in range(HEADS):
        lead = jnp.exp(-run_col[h])
        from_norm = jnp.sum(phiq[h].astype(F32) * norm_in[h : h + 1, :], axis=1, keepdims=True)
        inverse = 1.0 / (den[h] + lead * from_norm)
        o_ref[:, lanes(h)] = o_ref[:, lanes(h)] * inverse - t_ref[:, lanes(h)].astype(F32)
        den[h] = lead * inverse

    for m, c in enumerate([z] + other_z[::-1]):
        if m:
            copy(wout.at[0], cin.at[c], s_w.at[0], r_w.at[c], at_z(c)).wait_recv()
        for n, i in enumerate(other_x):
            send(cin.at[c], fin.at[x, c], s_v.at[n * NZ + m], r_v.at[x * NZ + c], at_x(i))

    def finish(p, carry, row_term):
        for e in range(PER_X):
            h = PER_X * p + e
            part = pl.ds(e * PER_HEAD, PER_HEAD)
            state = run[pl.ds(h, 1), :] * carry[part].reshape(T, T) + row_term[part].reshape(T, T)
            high = state.astype(BF16)
            low = (state - high.astype(F32)).astype(BF16)
            phi = phiq[h]
            o_ref[:, lanes(h)] = o_ref[:, lanes(h)] + den[h] * (dot(phi, high) + dot(phi, low))

    run[ROW, :] = decay_x
    for i in other_x:
        copy(before.at[0], term.at[i], s_t.at[0], r_t.at[i], at_x(i)).wait_recv()
    finish(x, cin, before.at[x])
    for p in other_x[::-1]:
        for c in range(NZ):
            copy(cin.at[0], fin.at[p, c], s_v.at[0], r_v.at[p * NZ + c], at_x(p)).wait_recv()
        finish(p, fin.at[p], term.at[p])

    for c in sent:
        c.wait_send()
    each_later(lambda i: aux_to(i).wait_send())
    each_later(lambda i: total_to(i).wait_send())
    for i in range(NZ):
        @pl.when(i != z)
        def _(i=i):
            carry_to(i).wait_send()


def local(query_rows, key_rows, value_rows, teacher, query_map, key_map, decay_rate):
    rows = query_rows.shape[1:]
    operands = (
        query_rows.reshape(rows),
        key_rows.reshape(rows),
        value_rows.reshape(rows),
        teacher.reshape(rows),
        jnp.swapaxes(query_map, 1, 2),
        jnp.swapaxes(key_map, 1, 2),
        decay_rate.reshape(decay_rate.shape[1:]),
    )
    dma = lambda n: pltpu.SemaphoreType.DMA((n,))
    part = lambda *lead: pltpu.VMEM(lead + (SLICE, T), F32)
    small = lambda *lead: pltpu.VMEM(lead + (T,), F32)
    out = pl.pallas_call(
        kernel,
        out_shape=jax.ShapeDtypeStruct(rows, F32),
        in_specs=[pl.BlockSpec(memory_space=pltpu.HBM)] * 7,
        out_specs=pl.BlockSpec(memory_space=pltpu.VMEM),
        scratch_shapes=[pltpu.VMEM(a.shape, a.dtype) for a in operands]
        + [
            part(NX, NZ), part(NX, NZ), part(NX, NZ), part(NX, NZ), part(NZ - 1), part(NZ), part(NG),
            part(NZ), part(NZ), part(NX, NZ),
            small(NX, HEADS), small(NX, HEADS), small(NZ, 2 * HEADS), small(NG, 2 * HEADS),
            pltpu.VMEM((HEADS, T, T), BF16), pltpu.VMEM((HEADS, T, T), BF16),
            small(2 * HEADS), small(HEADS, T), small(HEADS, T),
            dma(7), dma(NX - 1), dma(NX), dma(NX - 1), dma(NX), dma(NZ - 1), dma(NZ), dma(NG), dma(NG),
            dma((NX - 1) * NZ), dma(NX * NZ), dma(NZ - 1), dma(NZ), dma(NG), dma(NG),
            dma(NZ), dma(NZ), dma((NX - 1) * NZ), dma(NX * NZ), dma(NX - 1), dma(NX),
        ],
        compiler_params=pltpu.CompilerParams(
            collective_id=0, has_side_effects=True, vmem_limit_bytes=32 * 1024 * 1024
        ),
    )(*[pltpu.with_memory_space_constraint(a, pltpu.HBM) for a in operands])
    return out.reshape(query_rows.shape)


def solution(mesh):
    rows = P(None, ("grp", "seq"), None)
    return jax.shard_map(
        local,
        mesh=mesh,
        in_specs=(rows, rows, rows, rows, P(), P(), P(None, None, ("grp", "seq"))),
        out_specs=rows,
        check_vma=False,
    )
```

time: 43.4 us -> 36.2 us (0.83)
  the two profiles are of different devices: /device:TPU:1 before, /device:TPU:24 now
where the time goes in v1:
time: 36.2 us; the launch traced here: 36.1 us
  Pallas kernels  35.3 us (98%)
  local copies, waits for them, and re-layouts  0.8 us (2%)
    pallas_call x1, Pallas kernels, local(): pl.pallas_call(kernel, out_shape=jax.ShapeDtypeStruct(rows, F32), in_spec...  35.3 us
    unnamed x1, local copies, waits for them, and re-layouts  0.8 us

profile of v1, /device:TPU:24, one launch (start us, length us, event | category | flops | bytes accessed | tf_op | source)
XLA Modules:
  0.0 36.1 jit_solution(8544185525202066970)
XLA Ops:
  0.0 35.3 %shard_map.73 = f32[128,1024]{1,0:T(8,128)S(1)} custom-call(bf16[128,1024]{1,0:T(8,128)(2,1)} %bitcast.9, bf16[128,1024]{1,0:T(8,128)(2,1)} %bitcast.10, bf16[128,1024]{1,0:T(8,128)(2,1)} %bitcast.11, bf16[128,1024]{1,0:T(8,128)(2,1)} %bitcast.12, bf16[8,64,128]{2,1,0:T(8,128)(2,1)} %bitcast.13, bf16[8,64,128]{2,1,0:T(8,128)(2,1)} %bitcast.14, f32[8,128]{1,0:T(8,128)} %bitcast.15), custom_call_target="tpu_custom_call" | custom-call | tf_op jit(solution)/shard_map/pallas_call | solution.py:301
  35.3 0.8 %copy.9 = f32[1,128,1024]{2,1,0:T(8,128)} copy(f32[1,128,1024]{2,1,0:T(8,128)S(1)} %bitcast.8) | data formatting | bytes 1048576

commit v2 on v1

v2 whole, which is shorter than its diff:
```python
import jax
import jax.numpy as jnp
from jax import lax
from jax.experimental import pallas as pl
from jax.experimental.pallas import tpu as pltpu
from jax.sharding import PartitionSpec as P

MESH = pl.DeviceIdType.MESH
F32 = jnp.float32
BF16 = jnp.bfloat16

NX, NZ, NG = 4, 8, 8
HEADS = 8
T = 128
SLICE = HEADS * T // (NX * NZ)
PER_HEAD = T // SLICE
PER_X = HEADS // NX
AUX = 2 * HEADS
HALF = NZ // 2
SIDE = HALF * SLICE
QUARTER = 2 * SIDE + AUX


def dot(a, b, dims=((1,), (0,))):
    return lax.dot_general(a, b, (dims, ((), ())), preferred_element_type=F32)


def lanes(h):
    return pl.ds(h * T, T)


def slice_row(c):
    return c * SLICE + (c // HALF) * AUX


def kernel(
    q_hbm, k_hbm, v_hbm, t_hbm, wq_hbm, wk_hbm, rate_hbm, o_ref,
    q_ref, k_ref, v_ref, t_ref, wq_ref, wk_ref, rate_ref,
    own, xin, before, term, tout, zin, gin, wout, cin, fin,
    phiq, phik, run, run_col, den,
    s_in, s_x, r_x, s_z, r_z, s_g, r_g, s_w, r_w, s_v, r_v, s_t, r_t,
):
    g = lax.axis_index("grp")
    s = lax.axis_index("seq")
    z, x = s // NX, s % NX

    def at_x(i):
        return (g, z * NX + i)

    def at_z(i):
        return (g, i * NX + x)

    def at_g(i):
        return (i, s)

    def copy(src, dst, ssem, rsem, to):
        return pltpu.make_async_remote_copy(
            src_ref=src, dst_ref=dst, send_sem=ssem, recv_sem=rsem, device_id=to, device_id_type=MESH
        )

    other_x = [(x + d) % NX for d in (2, 1, 3)]
    other_z = [(z + d) % NZ for d in (4, 3, 5, 2, 6, 1, 7)]
    other_g = [(g + d) % NG for d in (4, 3, 5, 2, 6, 1, 7)]

    barrier = pltpu.get_barrier_semaphore()
    for to in [at_z(i) for i in other_z] + [at_g(i) for i in other_g] + [at_x(i) for i in other_x]:
        pl.semaphore_signal(barrier, inc=1, device_id=to, device_id_type=MESH)

    pairs = [
        (rate_hbm, rate_ref), (wk_hbm, wk_ref), (k_hbm, k_ref), (v_hbm, v_ref),
        (wq_hbm, wq_ref), (q_hbm, q_ref), (t_hbm, t_ref),
    ]
    loads = [pltpu.make_async_copy(a, b, s_in.at[n]) for n, (a, b) in enumerate(pairs)]
    for load in loads:
        load.start()

    loads[0].wait()
    lane = lax.broadcasted_iota(jnp.int32, (HEADS, T), 1)
    running = rate_ref[...]
    step = 1
    while step < T:
        running = running + jnp.where(lane >= step, pltpu.roll(running, step, 1), 0.0)
        step *= 2
    total = jnp.broadcast_to(running[:, T - 1 : T], (HEADS, T))
    run[pl.ds(0, HEADS), :] = running
    fades = jnp.exp(running - total)

    loads[1].wait()
    loads[2].wait()
    loads[3].wait()
    sums = []
    for h in range(HEADS):
        product = dot(wk_ref[h], k_ref[:, lanes(h)], ((1,), (1,)))
        both = jnp.log1p(jnp.exp(-jnp.abs(product)))
        phi = jnp.concatenate([jnp.maximum(product, 0.0) + both, jnp.maximum(-product, 0.0) + both], axis=0)
        phi = phi.astype(BF16)
        phik[h] = phi
        fade = fades[h : h + 1, :]
        faded = phi.astype(F32) * fade
        at = slice_row((h % PER_X) * PER_HEAD)
        own[h // PER_X, pl.ds(at, T), :] = dot(faded.astype(BF16), v_ref[:, lanes(h)])
        high = fade.astype(BF16)
        low = (fade - high.astype(F32)).astype(BF16)
        pair = dot(jnp.concatenate([high, low], axis=0), phi, ((1,), (1,)))
        sums.append(pair[0:1, :] + pair[1:2, :])
    aux = jnp.concatenate(sums + [jnp.exp(-total)], axis=0)
    for p in range(NX):
        own[p, pl.ds(SIDE, AUX), :] = aux

    pl.semaphore_wait(barrier, len(other_x) + len(other_z) + len(other_g))

    order = other_z + [z]

    def aux_to(i):
        at = pl.ds(SIDE, AUX)
        return copy(own.at[i, at], xin.at[x, at], s_x.at[0], r_x.at[NZ], at_x(i))

    def slice_at(c):
        return pl.ds(pl.multiple_of(slice_row(c), AUX), SLICE)

    def slice_to(i, c):
        at = slice_at(c)
        return copy(own.at[i, at], xin.at[x, at], s_x.at[0], r_x.at[c], at_x(i))

    for i in other_x:
        aux_to(i).start()
    for c in order:
        for i in other_x:
            slice_to(i, c).start()
    xin[x] = own[x]

    causal = lax.broadcasted_iota(jnp.int32, (T, T), 0) >= lax.broadcasted_iota(jnp.int32, (T, T), 1)

    def attend(start, end):
        for h in range(start, end):
            w = wq_ref[h]
            product = dot(q_ref[:, lanes(h)], jnp.concatenate([w, -w], axis=0), ((1,), (1,)))
            phi = (jnp.maximum(product, 0.0) + jnp.log1p(jnp.exp(-jnp.abs(product)))).astype(BF16)
            phiq[h] = phi
            row = run[pl.ds(h, 1), :]
            column = jnp.broadcast_to(row, (T, T)).T
            run_col[h] = column
            scores = dot(phi, phik[h])
            weighted = jnp.where(causal, scores * jnp.exp(row - column), 0.0)
            den[h] = jnp.broadcast_to(jnp.sum(weighted, axis=1, keepdims=True), (T, T))
            o_ref[:, lanes(h)] = dot(weighted.astype(BF16), v_ref[:, lanes(h)])

    loads[4].wait()
    loads[5].wait()
    loads[6].wait()
    attend(0, 4)

    def chain(ref, n, here, base):
        norm, decay = jnp.zeros((HEADS, T), F32), jnp.ones((HEADS, T), F32)
        norm_before, decay_before = norm, decay
        for i in range(n):
            norm_before = jnp.where(here == i, norm, norm_before)
            decay_before = jnp.where(here == i, decay, decay_before)
            d = ref[i, pl.ds(base + HEADS, HEADS), :]
            norm = d * norm + ref[i, pl.ds(base, HEADS), :]
            decay = d * decay
        return norm, decay, norm_before, decay_before

    def head_row(ref, i, base, c):
        return ref[i, pl.ds(base + HEADS + (x * NZ + c) // PER_HEAD, 1), :]

    def total_to_row(c):
        return copy(tout.at[c], zin.at[z], s_z.at[0], r_z.at[0], at_z(c))

    three = pl.ds(0, NX - 1)
    at = pl.ds(SIDE, AUX)
    copy(own.at[three, at], xin.at[three, at], s_x.at[0], r_x.at[NZ], at_x(other_x[0])).wait_recv()
    norm, decay, norm_x, decay_x = chain(xin, NX, x, SIDE)
    for c in order:
        at = slice_at(c)
        copy(own.at[three, at], xin.at[three, at], s_x.at[0], r_x.at[c], at_x(other_x[0])).wait_recv()
        acc = jnp.zeros((SLICE, T), F32)
        for i in range(NX):
            before[i, c] = acc
            acc = head_row(xin, i, SIDE, c) * acc + xin[i, at]
        tout[c, pl.ds(0, SLICE), :] = acc
        tout[c, pl.ds(SLICE, HEADS), :] = norm
        tout[c, pl.ds(SLICE + HEADS, HEADS), :] = decay

        @pl.when(c != z)
        def _(c=c):
            total_to_row(c).start()

    zin[z] = tout[z]
    for i in other_x:
        copy(before.at[i], term.at[x], s_t.at[0], r_t.at[0], at_x(i)).start()
    attend(4, 6)

    def each_later(act):
        for d in (4, 5, 3, 2, 6, 1, 7):
            @pl.when(g + d < NG)
            def _(d=d):
                act(g + d)

    def each_earlier(act):
        for i in range(NG - 1):
            @pl.when(i < g)
            def _(i=i):
                act(i)

    def total_to(i):
        return copy(gin.at[g], gin.at[g], s_g.at[i], r_g.at[g], at_g(i))

    seven = pl.ds(0, NZ - 1)
    copy(tout.at[seven], zin.at[seven], s_z.at[0], r_z.at[0], at_z(other_z[0])).wait_recv()
    acc = zin[0, pl.ds(0, SLICE), :]
    for i in range(1, NZ):
        acc = head_row(zin, i, SLICE, z) * acc + zin[i, pl.ds(0, SLICE), :]
    norm, decay, norm_z, decay_z = chain(zin, NZ, z, SLICE)
    gin[g, pl.ds(0, SLICE), :] = acc
    gin[g, pl.ds(SLICE, HEADS), :] = norm
    gin[g, pl.ds(SLICE + HEADS, HEADS), :] = decay
    each_later(lambda i: total_to(i).start())
    attend(6, HEADS)

    each_earlier(lambda i: copy(gin.at[g], gin.at[i], s_g.at[0], r_g.at[i], at_g(i)).wait_recv())
    acc = jnp.zeros((SLICE, T), F32)
    for i in range(NG - 1):
        acc = jnp.where(i < g, head_row(gin, i, SLICE, z) * acc + gin[i, pl.ds(0, SLICE), :], acc)

    def carry_to(i):
        return copy(wout.at[i], cin.at[z], s_w.at[0], r_w.at[z], at_z(i))

    for i in range(NZ):
        wout[i] = acc

        @pl.when(i != z)
        def _(i=i):
            carry_to(i).start()

        if i < NZ - 1:
            acc = head_row(zin, i, SLICE, z) * acc + zin[i, pl.ds(0, SLICE), :]
    cin[z] = wout[z]

    norm_g = jnp.zeros((HEADS, T), F32)
    for i in range(NG - 1):
        arrived = gin[i, pl.ds(SLICE + HEADS, HEADS), :] * norm_g + gin[i, pl.ds(SLICE, HEADS), :]
        norm_g = jnp.where(i < g, arrived, norm_g)
    norm_in = decay_x * (decay_z * norm_g + norm_z) + norm_x
    for h in range(HEADS):
        lead = jnp.exp(-run_col[h])
        from_norm = jnp.sum(phiq[h].astype(F32) * norm_in[h : h + 1, :], axis=1, keepdims=True)
        inverse = 1.0 / (den[h] + lead * from_norm)
        o_ref[:, lanes(h)] = o_ref[:, lanes(h)] * inverse - t_ref[:, lanes(h)].astype(F32)
        den[h] = lead * inverse
    run[pl.ds(HEADS, HEADS), :] = decay_x

    for m, c in enumerate([z] + other_z[::-1]):
        if m:
            copy(wout.at[0], cin.at[c], s_w.at[0], r_w.at[c], at_z(c)).wait_recv()
        for i in other_x:
            copy(cin.at[c], fin.at[x, c], s_v.at[0], r_v.at[x], at_x(i)).start()

    def finish(p, carry, row_term):
        for e in range(PER_X):
            h = PER_X * p + e
            part = pl.ds(e * PER_HEAD, PER_HEAD)
            state = run[pl.ds(HEADS + h, 1), :] * carry[part].reshape(T, T) + row_term[part].reshape(T, T)
            high = state.astype(BF16)
            low = (state - high.astype(F32)).astype(BF16)
            phi = phiq[h]
            at = pl.ds(pl.multiple_of(h * T, T), T)
            o_ref[:, at] = o_ref[:, at] + den[h] * (dot(phi, high) + dot(phi, low))

    copy(before.at[three], term.at[three], s_t.at[0], r_t.at[0], at_x(other_x[0])).wait_recv()
    finish(x, cin, before.at[x])
    for p in other_x[::-1]:
        copy(cin, fin.at[p], s_v.at[0], r_v.at[p], at_x(p)).wait_recv()
        finish(p, fin.at[p], term.at[p])

    to = at_x(other_x[0])
    copy(own.at[three], xin.at[three], s_x.at[0], r_x.at[0], to).wait_send()
    copy(before.at[three], term.at[three], s_t.at[0], r_t.at[0], to).wait_send()
    copy(fin.at[three], fin.at[three], s_v.at[0], r_v.at[0], to).wait_send()
    copy(tout.at[seven], zin.at[seven], s_z.at[0], r_z.at[0], at_z(other_z[0])).wait_send()
    copy(wout.at[seven], cin.at[seven], s_w.at[0], r_w.at[0], at_z(other_z[0])).wait_send()
    each_later(lambda i: total_to(i).wait_send())


def local(query_rows, key_rows, value_rows, teacher, query_map, key_map, decay_rate):
    rows = query_rows.shape[1:]
    operands = (
        query_rows.reshape(rows),
        key_rows.reshape(rows),
        value_rows.reshape(rows),
        teacher.reshape(rows),
        jnp.swapaxes(query_map, 1, 2),
        jnp.swapaxes(key_map, 1, 2),
        decay_rate.reshape(decay_rate.shape[1:]),
    )
    dma = lambda n: pltpu.SemaphoreType.DMA((n,))
    part = lambda *lead: pltpu.VMEM(lead + (SLICE, T), F32)
    rowed = lambda *lead: pltpu.VMEM(lead + (T,), F32)
    out = pl.pallas_call(
        kernel,
        out_shape=jax.ShapeDtypeStruct(rows, F32),
        in_specs=[pl.BlockSpec(memory_space=pltpu.HBM)] * 7,
        out_specs=pl.BlockSpec(memory_space=pltpu.VMEM),
        scratch_shapes=[pltpu.VMEM(a.shape, a.dtype) for a in operands]
        + [
            rowed(NX, QUARTER), rowed(NX, QUARTER), part(NX, NZ), part(NX, NZ),
            rowed(NZ, SLICE + AUX), rowed(NZ, SLICE + AUX), rowed(NG, SLICE + AUX),
            part(NZ), part(NZ), part(NX, NZ),
            pltpu.VMEM((HEADS, T, T), BF16), pltpu.VMEM((HEADS, T, T), BF16),
            rowed(2 * HEADS), rowed(HEADS, T), rowed(HEADS, T),
            dma(7), dma(1), dma(NZ + 1), dma(1), dma(1), dma(NG), dma(NG),
            dma(1), dma(NZ), dma(1), dma(NX), dma(1), dma(1),
        ],
        compiler_params=pltpu.CompilerParams(
            collective_id=0, has_side_effects=True, vmem_limit_bytes=32 * 1024 * 1024
        ),
    )(*[pltpu.with_memory_space_constraint(a, pltpu.HBM) for a in operands])
    return out.reshape(query_rows.shape)


def solution(mesh):
    rows = P(None, ("grp", "seq"), None)
    return jax.shard_map(
        local,
        mesh=mesh,
        in_specs=(rows, rows, rows, rows, P(), P(), P(None, None, ("grp", "seq"))),
        out_specs=rows,
        check_vma=False,
    )
```

time: 36.2 us -> 34.7 us (0.959)
  Pallas kernels: 35.3 us -> 33.8 us
    pallas_call x1, Pallas kernels: 35.3 us -> 33.8 us  [local(): pl.pallas_call(kernel, out_shape=jax.ShapeDtypeStruct(rows, F32), in_spec...]
where the time goes in v2:
time: 34.7 us; the launch traced here: 34.6 us
  Pallas kernels  33.8 us (97%)
  local copies, waits for them, and re-layouts  0.8 us (2%)
    pallas_call x1, Pallas kernels, local(): pl.pallas_call(kernel, out_shape=jax.ShapeDtypeStruct(rows, F32), in_spec...  33.8 us
    unnamed x1, local copies, waits for them, and re-layouts  0.8 us

profile of v2, /device:TPU:24, one launch (start us, length us, event | category | flops | bytes accessed | tf_op | source)
XLA Modules:
  0.0 34.6 jit_solution(9264860815474218558)
XLA Ops:
  0.0 33.8 %shard_map.73 = f32[128,1024]{1,0:T(8,128)S(1)} custom-call(bf16[128,1024]{1,0:T(8,128)(2,1)} %bitcast.9, bf16[128,1024]{1,0:T(8,128)(2,1)} %bitcast.10, bf16[128,1024]{1,0:T(8,128)(2,1)} %bitcast.11, bf16[128,1024]{1,0:T(8,128)(2,1)} %bitcast.12, bf16[8,64,128]{2,1,0:T(8,128)(2,1)} %bitcast.13, bf16[8,64,128]{2,1,0:T(8,128)(2,1)} %bitcast.14, f32[8,128]{1,0:T(8,128)} %bitcast.15), custom_call_target="tpu_custom_call" | custom-call | tf_op jit(solution)/shard_map/pallas_call | solution.py:299
  33.8 0.8 %copy.9 = f32[1,128,1024]{2,1,0:T(8,128)} copy(f32[1,128,1024]{2,1,0:T(8,128)S(1)} %bitcast.8) | data formatting | bytes 1048576

commit v3 on v2

--- a/solution.py
+++ b/solution.py
@@ -36,9 +36,9 @@
 def kernel(
     q_hbm, k_hbm, v_hbm, t_hbm, wq_hbm, wk_hbm, rate_hbm, o_ref,
     q_ref, k_ref, v_ref, t_ref, wq_ref, wk_ref, rate_ref,
-    own, xin, before, term, tout, zin, gin, wout, cin, fin,
+    own, xin, tout, zin, gin, auxz, auxg, wout, cin, vout, fin,
     phiq, phik, run, run_col, den,
-    s_in, s_x, r_x, s_z, r_z, s_g, r_g, s_w, r_w, s_v, r_v, s_t, r_t,
+    s_in, s_az, r_az, s_ag, r_ag, s_x, r_x, s_z, r_z, s_g, r_g, s_w, r_w, s_v, r_v,
 ):
     g = lax.axis_index("grp")
     s = lax.axis_index("seq")
@@ -109,7 +109,12 @@
 
     pl.semaphore_wait(barrier, len(other_x) + len(other_z) + len(other_g))
 
-    order = other_z + [z]
+    odd = z % 2
+
+    def slots(even_row, odd_row):
+        return [(z + jnp.where(odd == 1, b, a)) % NZ for a, b in zip(even_row, odd_row)]
+
+    order = slots((4, 2, 6, 0, 3, 5, 1, 7), (3, 5, 1, 7, 4, 2, 6, 0))
 
     def aux_to(i):
         at = pl.ds(SIDE, AUX)
@@ -171,24 +176,23 @@
     at = pl.ds(SIDE, AUX)
     copy(own.at[three, at], xin.at[three, at], s_x.at[0], r_x.at[NZ], at_x(other_x[0])).wait_recv()
     norm, decay, norm_x, decay_x = chain(xin, NX, x, SIDE)
+    auxz[z, pl.ds(0, HEADS), :] = norm
+    auxz[z, pl.ds(HEADS, HEADS), :] = decay
+    for i in other_z:
+        copy(auxz.at[z], auxz.at[z], s_az.at[0], r_az.at[0], at_z(i)).start()
     for c in order:
         at = slice_at(c)
         copy(own.at[three, at], xin.at[three, at], s_x.at[0], r_x.at[c], at_x(other_x[0])).wait_recv()
-        acc = jnp.zeros((SLICE, T), F32)
-        for i in range(NX):
-            before[i, c] = acc
+        acc = xin[0, at]
+        for i in range(1, NX):
             acc = head_row(xin, i, SIDE, c) * acc + xin[i, at]
-        tout[c, pl.ds(0, SLICE), :] = acc
-        tout[c, pl.ds(SLICE, HEADS), :] = norm
-        tout[c, pl.ds(SLICE + HEADS, HEADS), :] = decay
+        tout[c] = acc
 
         @pl.when(c != z)
         def _(c=c):
             total_to_row(c).start()
 
     zin[z] = tout[z]
-    for i in other_x:
-        copy(before.at[i], term.at[x], s_t.at[0], r_t.at[0], at_x(i)).start()
     attend(4, 6)
 
     def each_later(act):
@@ -203,43 +207,46 @@
             def _(i=i):
                 act(i)
 
+    def sums_to(i):
+        return copy(auxg.at[g], auxg.at[g], s_ag.at[i], r_ag.at[g], at_g(i))
+
     def total_to(i):
         return copy(gin.at[g], gin.at[g], s_g.at[i], r_g.at[g], at_g(i))
 
     seven = pl.ds(0, NZ - 1)
+    copy(auxz.at[seven], auxz.at[seven], s_az.at[0], r_az.at[0], at_z(other_z[0])).wait_recv()
+    norm, decay, norm_z, decay_z = chain(auxz, NZ, z, 0)
+    auxg[g, pl.ds(0, HEADS), :] = norm
+    auxg[g, pl.ds(HEADS, HEADS), :] = decay
+    each_later(lambda i: sums_to(i).start())
     copy(tout.at[seven], zin.at[seven], s_z.at[0], r_z.at[0], at_z(other_z[0])).wait_recv()
-    acc = zin[0, pl.ds(0, SLICE), :]
+    acc = zin[0]
     for i in range(1, NZ):
-        acc = head_row(zin, i, SLICE, z) * acc + zin[i, pl.ds(0, SLICE), :]
-    norm, decay, norm_z, decay_z = chain(zin, NZ, z, SLICE)
-    gin[g, pl.ds(0, SLICE), :] = acc
-    gin[g, pl.ds(SLICE, HEADS), :] = norm
-    gin[g, pl.ds(SLICE + HEADS, HEADS), :] = decay
+        acc = head_row(auxz, i, 0, z) * acc + zin[i]
+    gin[g] = acc
     each_later(lambda i: total_to(i).start())
     attend(6, HEADS)
 
-    each_earlier(lambda i: copy(gin.at[g], gin.at[i], s_g.at[0], r_g.at[i], at_g(i)).wait_recv())
+    each_earlier(lambda i: copy(auxg.at[g], auxg.at[i], s_ag.at[i], r_ag.at[i], at_g(i)).wait_recv())
+    each_earlier(lambda i: copy(gin.at[g], gin.at[i], s_g.at[i], r_g.at[i], at_g(i)).wait_recv())
     acc = jnp.zeros((SLICE, T), F32)
     for i in range(NG - 1):
-        acc = jnp.where(i < g, head_row(gin, i, SLICE, z) * acc + gin[i, pl.ds(0, SLICE), :], acc)
+        acc = jnp.where(i < g, head_row(auxg, i, 0, z) * acc + gin[i], acc)
 
     def carry_to(i):
         return copy(wout.at[i], cin.at[z], s_w.at[0], r_w.at[z], at_z(i))
 
     for i in range(NZ):
         wout[i] = acc
-
-        @pl.when(i != z)
-        def _(i=i):
-            carry_to(i).start()
-
         if i < NZ - 1:
-            acc = head_row(zin, i, SLICE, z) * acc + zin[i, pl.ds(0, SLICE), :]
+            acc = head_row(auxz, i, 0, z) * acc + zin[i]
+    for d in (1, 7, 2, 6, 3, 5, 4):
+        carry_to((z + d) % NZ).start()
     cin[z] = wout[z]
 
     norm_g = jnp.zeros((HEADS, T), F32)
     for i in range(NG - 1):
-        arrived = gin[i, pl.ds(SLICE + HEADS, HEADS), :] * norm_g + gin[i, pl.ds(SLICE, HEADS), :]
+        arrived = auxg[i, pl.ds(HEADS, HEADS), :] * norm_g + auxg[i, pl.ds(0, HEADS), :]
         norm_g = jnp.where(i < g, arrived, norm_g)
     norm_in = decay_x * (decay_z * norm_g + norm_z) + norm_x
     for h in range(HEADS):
@@ -248,38 +255,44 @@
         inverse = 1.0 / (den[h] + lead * from_norm)
         o_ref[:, lanes(h)] = o_ref[:, lanes(h)] * inverse - t_ref[:, lanes(h)].astype(F32)
         den[h] = lead * inverse
-    run[pl.ds(HEADS, HEADS), :] = decay_x
-
-    for m, c in enumerate([z] + other_z[::-1]):
-        if m:
+
+    for c in slots((0, 2, 6, 4, 1, 7, 3, 5), (1, 7, 3, 5, 0, 2, 6, 4)):
+        @pl.when(c != z)
+        def _(c=c):
             copy(wout.at[0], cin.at[c], s_w.at[0], r_w.at[c], at_z(c)).wait_recv()
+
+        at = slice_at(c)
+        acc = cin[c]
+        for i in range(NX):
+            vout[i, c] = acc
+            if i < NX - 1:
+                acc = head_row(xin, i, SIDE, c) * acc + xin[i, at]
         for i in other_x:
-            copy(cin.at[c], fin.at[x, c], s_v.at[0], r_v.at[x], at_x(i)).start()
-
-    def finish(p, carry, row_term):
+            copy(vout.at[i, c], fin.at[x, c], s_v.at[0], r_v.at[x], at_x(i)).start()
+
+    def finish(p, states):
         for e in range(PER_X):
             h = PER_X * p + e
-            part = pl.ds(e * PER_HEAD, PER_HEAD)
-            state = run[pl.ds(HEADS + h, 1), :] * carry[part].reshape(T, T) + row_term[part].reshape(T, T)
+            state = states[pl.ds(e * PER_HEAD, PER_HEAD)].reshape(T, T)
             high = state.astype(BF16)
             low = (state - high.astype(F32)).astype(BF16)
             phi = phiq[h]
             at = pl.ds(pl.multiple_of(h * T, T), T)
             o_ref[:, at] = o_ref[:, at] + den[h] * (dot(phi, high) + dot(phi, low))
 
-    copy(before.at[three], term.at[three], s_t.at[0], r_t.at[0], at_x(other_x[0])).wait_recv()
-    finish(x, cin, before.at[x])
+    finish(x, vout.at[x])
     for p in other_x[::-1]:
-        copy(cin, fin.at[p], s_v.at[0], r_v.at[p], at_x(p)).wait_recv()
-        finish(p, fin.at[p], term.at[p])
+        copy(vout.at[0], fin.at[p], s_v.at[0], r_v.at[p], at_x(p)).wait_recv()
+        finish(p, fin.at[p])
 
     to = at_x(other_x[0])
     copy(own.at[three], xin.at[three], s_x.at[0], r_x.at[0], to).wait_send()
-    copy(before.at[three], term.at[three], s_t.at[0], r_t.at[0], to).wait_send()
-    copy(fin.at[three], fin.at[three], s_v.at[0], r_v.at[0], to).wait_send()
+    copy(vout.at[three], fin.at[three], s_v.at[0], r_v.at[0], to).wait_send()
     copy(tout.at[seven], zin.at[seven], s_z.at[0], r_z.at[0], at_z(other_z[0])).wait_send()
     copy(wout.at[seven], cin.at[seven], s_w.at[0], r_w.at[0], at_z(other_z[0])).wait_send()
     each_later(lambda i: total_to(i).wait_send())
+    each_later(lambda i: sums_to(i).wait_send())
+    copy(auxz.at[seven], auxz.at[seven], s_az.at[0], r_az.at[0], at_z(other_z[0])).wait_send()
 
 
 def local(query_rows, key_rows, value_rows, teacher, query_map, key_map, decay_rate):
@@ -303,13 +316,13 @@
         out_specs=pl.BlockSpec(memory_space=pltpu.VMEM),
         scratch_shapes=[pltpu.VMEM(a.shape, a.dtype) for a in operands]
         + [
-            rowed(NX, QUARTER), rowed(NX, QUARTER), part(NX, NZ), part(NX, NZ),
-            rowed(NZ, SLICE + AUX), rowed(NZ, SLICE + AUX), rowed(NG, SLICE + AUX),
-            part(NZ), part(NZ), part(NX, NZ),
+            rowed(NX, QUARTER), rowed(NX, QUARTER),
+            part(NZ), part(NZ), part(NG), rowed(NZ, AUX), rowed(NG, AUX),
+            part(NZ), part(NZ), part(NX, NZ), part(NX, NZ),
             pltpu.VMEM((HEADS, T, T), BF16), pltpu.VMEM((HEADS, T, T), BF16),
-            rowed(2 * HEADS), rowed(HEADS, T), rowed(HEADS, T),
-            dma(7), dma(1), dma(NZ + 1), dma(1), dma(1), dma(NG), dma(NG),
-            dma(1), dma(NZ), dma(1), dma(NX), dma(1), dma(1),
+            rowed(HEADS), rowed(HEADS, T), rowed(HEADS, T),
+            dma(7), dma(1), dma(1), dma(NG), dma(NG), dma(1), dma(NZ + 1), dma(1), dma(1), dma(NG), dma(NG),
+            dma(1), dma(NZ), dma(1), dma(NX),
         ],
         compiler_params=pltpu.CompilerParams(
             collective_id=0, has_side_effects=True, vmem_limit_bytes=32 * 1024 * 1024

time: 34.7 us -> 33.3 us (0.960)
  Pallas kernels: 33.8 us -> 32.3 us
    pallas_call x1, Pallas kernels: 33.8 us -> 32.3 us  [local(): pl.pallas_call(kernel, out_shape=jax.ShapeDtypeStruct(rows, F32), in_spec...]
where the time goes in v3:
time: 33.3 us; the launch traced here: 33.1 us
  Pallas kernels  32.3 us (97%)
  local copies, waits for them, and re-layouts  0.8 us (2%)
    pallas_call x1, Pallas kernels, local(): pl.pallas_call(kernel, out_shape=jax.ShapeDtypeStruct(rows, F32), in_spec...  32.3 us
    unnamed x1, local copies, waits for them, and re-layouts  0.8 us

profile of v3, /device:TPU:24, one launch (start us, length us, event | category | flops | bytes accessed | tf_op | source)
XLA Modules:
  0.0 33.1 jit_solution(954025074448522325)
XLA Ops:
  0.0 32.3 %shard_map.73 = f32[128,1024]{1,0:T(8,128)S(1)} custom-call(bf16[128,1024]{1,0:T(8,128)(2,1)} %bitcast.9, bf16[128,1024]{1,0:T(8,128)(2,1)} %bitcast.10, bf16[128,1024]{1,0:T(8,128)(2,1)} %bitcast.11, bf16[128,1024]{1,0:T(8,128)(2,1)} %bitcast.12, bf16[8,64,128]{2,1,0:T(8,128)(2,1)} %bitcast.13, bf16[8,64,128]{2,1,0:T(8,128)(2,1)} %bitcast.14, f32[8,128]{1,0:T(8,128)} %bitcast.15), custom_call_target="tpu_custom_call" | custom-call | tf_op jit(solution)/shard_map/pallas_call | solution.py:312
  32.3 0.8 %copy.9 = f32[1,128,1024]{2,1,0:T(8,128)} copy(f32[1,128,1024]{2,1,0:T(8,128)S(1)} %bitcast.8) | data formatting | bytes 1048576

commit v4 on v3

--- a/solution.py
+++ b/solution.py
@@ -19,6 +19,26 @@
 HALF = NZ // 2
 SIDE = HALF * SLICE
 QUARTER = 2 * SIDE + AUX
+OUTWARD = (
+    (4, 2, 6, 3, 5, 1, 7, 0),
+    (4, 6, 0, 2, 5, 3, 7, 1),
+    (6, 0, 4, 5, 7, 1, 3, 2),
+    (0, 6, 2, 4, 7, 1, 5, 3),
+    (0, 2, 6, 1, 7, 3, 5, 4),
+    (0, 2, 4, 6, 1, 3, 7, 5),
+    (2, 0, 4, 1, 3, 5, 7, 6),
+    (2, 4, 0, 6, 3, 1, 5, 7),
+)
+INWARD = (
+    (0, 2, 6, 4, 1, 7, 3, 5),
+    (0, 2, 4, 6, 1, 3, 7, 5),
+    (2, 0, 4, 6, 1, 3, 5, 7),
+    (2, 4, 0, 6, 3, 1, 5, 7),
+    (4, 2, 6, 0, 3, 5, 1, 7),
+    (4, 6, 0, 2, 5, 3, 7, 1),
+    (6, 0, 4, 2, 5, 7, 1, 3),
+    (0, 6, 2, 4, 7, 1, 5, 3),
+)
 
 
 def dot(a, b, dims=((1,), (0,))):
@@ -59,11 +79,12 @@
         )
 
     other_x = [(x + d) % NX for d in (2, 1, 3)]
+    low_x = [jnp.where(x <= n, n + 1, n) for n in range(NX - 1)]
     other_z = [(z + d) % NZ for d in (4, 3, 5, 2, 6, 1, 7)]
     other_g = [(g + d) % NG for d in (4, 3, 5, 2, 6, 1, 7)]
 
     barrier = pltpu.get_barrier_semaphore()
-    for to in [at_z(i) for i in other_z] + [at_g(i) for i in other_g] + [at_x(i) for i in other_x]:
+    for to in [at_x(i) for i in other_x] + [at_z(i) for i in other_z] + [at_g(i) for i in other_g]:
         pl.semaphore_signal(barrier, inc=1, device_id=to, device_id_type=MESH)
 
     pairs = [
@@ -109,12 +130,16 @@
 
     pl.semaphore_wait(barrier, len(other_x) + len(other_z) + len(other_g))
 
-    odd = z % 2
-
-    def slots(even_row, odd_row):
-        return [(z + jnp.where(odd == 1, b, a)) % NZ for a, b in zip(even_row, odd_row)]
-
-    order = slots((4, 2, 6, 0, 3, 5, 1, 7), (3, 5, 1, 7, 4, 2, 6, 0))
+    def slots(table):
+        def one(column):
+            c = column[0]
+            for i in range(1, NZ):
+                c = jnp.where(z == i, column[i], c)
+            return c
+
+        return [one([row[n] for row in table]) for n in range(NZ)]
+
+    order = slots(OUTWARD)
 
     def aux_to(i):
         at = pl.ds(SIDE, AUX)
@@ -193,7 +218,6 @@
             total_to_row(c).start()
 
     zin[z] = tout[z]
-    attend(4, 6)
 
     def each_later(act):
         for d in (4, 5, 3, 2, 6, 1, 7):
@@ -225,7 +249,7 @@
         acc = head_row(auxz, i, 0, z) * acc + zin[i]
     gin[g] = acc
     each_later(lambda i: total_to(i).start())
-    attend(6, HEADS)
+    attend(4, HEADS)
 
     each_earlier(lambda i: copy(auxg.at[g], auxg.at[i], s_ag.at[i], r_ag.at[i], at_g(i)).wait_recv())
     each_earlier(lambda i: copy(gin.at[g], gin.at[i], s_g.at[i], r_g.at[i], at_g(i)).wait_recv())
@@ -236,13 +260,40 @@
     def carry_to(i):
         return copy(wout.at[i], cin.at[z], s_w.at[0], r_w.at[z], at_z(i))
 
-    for i in range(NZ):
+    wout[0] = acc
+
+    @pl.when(z != 0)
+    def _():
+        carry_to(0).start()
+
+    for i in range(1, NZ):
+        acc = head_row(auxz, i - 1, 0, z) * acc + zin[i - 1]
         wout[i] = acc
-        if i < NZ - 1:
-            acc = head_row(auxz, i, 0, z) * acc + zin[i]
-    for d in (1, 7, 2, 6, 3, 5, 4):
-        carry_to((z + d) % NZ).start()
+    for i in range(1, NZ):
+        @pl.when(i != z)
+        def _(i=i):
+            carry_to(i).start()
+
     cin[z] = wout[z]
+
+    inward = slots(INWARD)
+
+    def forward(c):
+        @pl.when(c != z)
+        def _(c=c):
+            copy(wout.at[0], cin.at[c], s_w.at[0], r_w.at[c], at_z(c)).wait_recv()
+
+        at = slice_at(c)
+        acc = cin[c]
+        for i in range(NX):
+            vout[i, c] = acc
+            if i < NX - 1:
+                acc = head_row(xin, i, SIDE, c) * acc + xin[i, at]
+        for i in low_x:
+            copy(vout.at[i, c], fin.at[x, c], s_v.at[0], r_v.at[x], at_x(i)).start()
+
+    for c in inward[:HALF]:
+        forward(c)
 
     norm_g = jnp.zeros((HEADS, T), F32)
     for i in range(NG - 1):
@@ -256,19 +307,8 @@
         o_ref[:, lanes(h)] = o_ref[:, lanes(h)] * inverse - t_ref[:, lanes(h)].astype(F32)
         den[h] = lead * inverse
 
-    for c in slots((0, 2, 6, 4, 1, 7, 3, 5), (1, 7, 3, 5, 0, 2, 6, 4)):
-        @pl.when(c != z)
-        def _(c=c):
-            copy(wout.at[0], cin.at[c], s_w.at[0], r_w.at[c], at_z(c)).wait_recv()
-
-        at = slice_at(c)
-        acc = cin[c]
-        for i in range(NX):
-            vout[i, c] = acc
-            if i < NX - 1:
-                acc = head_row(xin, i, SIDE, c) * acc + xin[i, at]
-        for i in other_x:
-            copy(vout.at[i, c], fin.at[x, c], s_v.at[0], r_v.at[x], at_x(i)).start()
+    for c in inward[HALF:]:
+        forward(c)
 
     def finish(p, states):
         for e in range(PER_X):
@@ -278,10 +318,11 @@
             low = (state - high.astype(F32)).astype(BF16)
             phi = phiq[h]
             at = pl.ds(pl.multiple_of(h * T, T), T)
-            o_ref[:, at] = o_ref[:, at] + den[h] * (dot(phi, high) + dot(phi, low))
+            product = dot(jnp.concatenate([phi, phi], axis=1), jnp.concatenate([high, low], axis=0))
+            o_ref[:, at] = o_ref[:, at] + den[h] * product
 
     finish(x, vout.at[x])
-    for p in other_x[::-1]:
+    for p in (other_x[1], other_x[2], other_x[0]):
         copy(vout.at[0], fin.at[p], s_v.at[0], r_v.at[p], at_x(p)).wait_recv()
         finish(p, fin.at[p])
 

time: 33.3 us -> 32.9 us (0.988)
  no operation moved by 1% of the time
where the time goes in v4:
time: 32.9 us; the launch traced here: 32.8 us
  Pallas kernels  32 us (97%)
  local copies, waits for them, and re-layouts  0.8 us (2%)
    pallas_call x1, Pallas kernels, local(): pl.pallas_call(kernel, out_shape=jax.ShapeDtypeStruct(rows, F32), in_spec...  32 us
    unnamed x1, local copies, waits for them, and re-layouts  0.8 us

profile of v4, /device:TPU:24, one launch (start us, length us, event | category | flops | bytes accessed | tf_op | source)
XLA Modules:
  0.0 32.8 jit_solution(9297958809341908547)
XLA Ops:
  0.0 32.0 %shard_map.73 = f32[128,1024]{1,0:T(8,128)S(1)} custom-call(bf16[128,1024]{1,0:T(8,128)(2,1)} %bitcast.9, bf16[128,1024]{1,0:T(8,128)(2,1)} %bitcast.10, bf16[128,1024]{1,0:T(8,128)(2,1)} %bitcast.11, bf16[128,1024]{1,0:T(8,128)(2,1)} %bitcast.12, bf16[8,64,128]{2,1,0:T(8,128)(2,1)} %bitcast.13, bf16[8,64,128]{2,1,0:T(8,128)(2,1)} %bitcast.14, f32[8,128]{1,0:T(8,128)} %bitcast.15), custom_call_target="tpu_custom_call" | custom-call | tf_op jit(solution)/shard_map/pallas_call | solution.py:353
  32.0 0.8 %copy.9 = f32[1,128,1024]{2,1,0:T(8,128)} copy(f32[1,128,1024]{2,1,0:T(8,128)S(1)} %bitcast.8) | data formatting | bytes 1048576

commit v5 on v4

--- a/solution.py
+++ b/solution.py
@@ -225,17 +225,31 @@
             def _(d=d):
                 act(g + d)
 
-    def each_earlier(act):
-        for i in range(NG - 1):
-            @pl.when(i < g)
-            def _(i=i):
-                act(i)
+    def from_earlier(act):
+        for n in range(1, NG):
+            @pl.when(g == n)
+            def _(n=n):
+                act(n)
+
+    def to_later(act):
+        for n in range(1, NG):
+            @pl.when(g == NG - 1 - n)
+            def _(n=n):
+                act(n)
+
+    def sums_of(n):
+        some = pl.ds(0, n)
+        return copy(auxg.at[some], auxg.at[some], s_ag.at[0], r_ag.at[0], at_g(other_g[0]))
+
+    def totals_of(n):
+        some = pl.ds(0, n)
+        return copy(gin.at[some], gin.at[some], s_g.at[0], r_g.at[0], at_g(other_g[0]))
 
     def sums_to(i):
-        return copy(auxg.at[g], auxg.at[g], s_ag.at[i], r_ag.at[g], at_g(i))
+        return copy(auxg.at[g], auxg.at[g], s_ag.at[0], r_ag.at[0], at_g(i))
 
     def total_to(i):
-        return copy(gin.at[g], gin.at[g], s_g.at[i], r_g.at[g], at_g(i))
+        return copy(gin.at[g], gin.at[g], s_g.at[0], r_g.at[0], at_g(i))
 
     seven = pl.ds(0, NZ - 1)
     copy(auxz.at[seven], auxz.at[seven], s_az.at[0], r_az.at[0], at_z(other_z[0])).wait_recv()
@@ -251,8 +265,8 @@
     each_later(lambda i: total_to(i).start())
     attend(4, HEADS)
 
-    each_earlier(lambda i: copy(auxg.at[g], auxg.at[i], s_ag.at[i], r_ag.at[i], at_g(i)).wait_recv())
-    each_earlier(lambda i: copy(gin.at[g], gin.at[i], s_g.at[i], r_g.at[i], at_g(i)).wait_recv())
+    from_earlier(lambda n: sums_of(n).wait_recv())
+    from_earlier(lambda n: totals_of(n).wait_recv())
     acc = jnp.zeros((SLICE, T), F32)
     for i in range(NG - 1):
         acc = jnp.where(i < g, head_row(auxg, i, 0, z) * acc + gin[i], acc)
@@ -331,8 +345,8 @@
     copy(vout.at[three], fin.at[three], s_v.at[0], r_v.at[0], to).wait_send()
     copy(tout.at[seven], zin.at[seven], s_z.at[0], r_z.at[0], at_z(other_z[0])).wait_send()
     copy(wout.at[seven], cin.at[seven], s_w.at[0], r_w.at[0], at_z(other_z[0])).wait_send()
-    each_later(lambda i: total_to(i).wait_send())
-    each_later(lambda i: sums_to(i).wait_send())
+    to_later(lambda n: totals_of(n).wait_send())
+    to_later(lambda n: sums_of(n).wait_send())
     copy(auxz.at[seven], auxz.at[seven], s_az.at[0], r_az.at[0], at_z(other_z[0])).wait_send()
 
 
@@ -362,7 +376,7 @@
             part(NZ), part(NZ), part(NX, NZ), part(NX, NZ),
             pltpu.VMEM((HEADS, T, T), BF16), pltpu.VMEM((HEADS, T, T), BF16),
             rowed(HEADS), rowed(HEADS, T), rowed(HEADS, T),
-            dma(7), dma(1), dma(1), dma(NG), dma(NG), dma(1), dma(NZ + 1), dma(1), dma(1), dma(NG), dma(NG),
+            dma(7), dma(1), dma(1), dma(1), dma(1), dma(1), dma(NZ + 1), dma(1), dma(1), dma(1), dma(1),
             dma(1), dma(NZ), dma(1), dma(NX),
         ],
         compiler_params=pltpu.CompilerParams(

time: 32.9 us -> 32.6 us (level)
  no operation moved by 1% of the time
where the time goes in v5:
time: 32.6 us; the launch traced here: 32.5 us
  Pallas kernels  31.7 us (97%)
  local copies, waits for them, and re-layouts  0.8 us (2%)
    pallas_call x1, Pallas kernels, local(): pl.pallas_call(kernel, out_shape=jax.ShapeDtypeStruct(rows, F32), in_spec...  31.7 us
    unnamed x1, local copies, waits for them, and re-layouts  0.8 us

profile of v5, /device:TPU:24, one launch (start us, length us, event | category | flops | bytes accessed | tf_op | source)
XLA Modules:
  0.0 32.5 jit_solution(5097072009014450286)
XLA Ops:
  0.0 31.7 %shard_map.73 = f32[128,1024]{1,0:T(8,128)S(1)} custom-call(bf16[128,1024]{1,0:T(8,128)(2,1)} %bitcast.9, bf16[128,1024]{1,0:T(8,128)(2,1)} %bitcast.10, bf16[128,1024]{1,0:T(8,128)(2,1)} %bitcast.11, bf16[128,1024]{1,0:T(8,128)(2,1)} %bitcast.12, bf16[8,64,128]{2,1,0:T(8,128)(2,1)} %bitcast.13, bf16[8,64,128]{2,1,0:T(8,128)(2,1)} %bitcast.14, f32[8,128]{1,0:T(8,128)} %bitcast.15), custom_call_target="tpu_custom_call" | custom-call | tf_op jit(solution)/shard_map/pallas_call | solution.py:367
  31.7 0.8 %copy.9 = f32[1,128,1024]{2,1,0:T(8,128)} copy(f32[1,128,1024]{2,1,0:T(8,128)S(1)} %bitcast.8) | data formatting | bytes 1048576

commit v6 on v5

--- a/solution.py
+++ b/solution.py
@@ -84,8 +84,12 @@
     other_g = [(g + d) % NG for d in (4, 3, 5, 2, 6, 1, 7)]
 
     barrier = pltpu.get_barrier_semaphore()
-    for to in [at_x(i) for i in other_x] + [at_z(i) for i in other_z] + [at_g(i) for i in other_g]:
+    for to in [at_x(i) for i in other_x] + [at_z(i) for i in other_z]:
         pl.semaphore_signal(barrier, inc=1, device_id=to, device_id_type=MESH)
+    for i in range(NG - 1):
+        @pl.when(i < g)
+        def _(i=i):
+            pl.semaphore_signal(barrier, inc=1, device_id=at_g(i), device_id_type=MESH)
 
     pairs = [
         (rate_hbm, rate_ref), (wk_hbm, wk_ref), (k_hbm, k_ref), (v_hbm, v_ref),
@@ -128,7 +132,7 @@
     for p in range(NX):
         own[p, pl.ds(SIDE, AUX), :] = aux
 
-    pl.semaphore_wait(barrier, len(other_x) + len(other_z) + len(other_g))
+    pl.semaphore_wait(barrier, NX - 1 + NZ - 1 + NG - 1 - g)
 
     def slots(table):
         def one(column):

time: 32.6 us -> 32.6 us (level)
  no operation moved by 1% of the time
where the time goes in v6:
time: 32.6 us; the launch traced here: 32.5 us
  Pallas kernels  31.7 us (97%)
  local copies, waits for them, and re-layouts  0.8 us (2%)
    pallas_call x1, Pallas kernels, local(): pl.pallas_call(kernel, out_shape=jax.ShapeDtypeStruct(rows, F32), in_spec...  31.7 us
    unnamed x1, local copies, waits for them, and re-layouts  0.8 us

profile of v6, /device:TPU:24, one launch (start us, length us, event | category | flops | bytes accessed | tf_op | source)
XLA Modules:
  0.0 32.5 jit_solution(735657690115855974)
XLA Ops:
  0.0 31.7 %shard_map.73 = f32[128,1024]{1,0:T(8,128)S(1)} custom-call(bf16[128,1024]{1,0:T(8,128)(2,1)} %bitcast.9, bf16[128,1024]{1,0:T(8,128)(2,1)} %bitcast.10, bf16[128,1024]{1,0:T(8,128)(2,1)} %bitcast.11, bf16[128,1024]{1,0:T(8,128)(2,1)} %bitcast.12, bf16[8,64,128]{2,1,0:T(8,128)(2,1)} %bitcast.13, bf16[8,64,128]{2,1,0:T(8,128)(2,1)} %bitcast.14, f32[8,128]{1,0:T(8,128)} %bitcast.15), custom_call_target="tpu_custom_call" | custom-call | tf_op jit(solution)/shard_map/pallas_call | solution.py:371
  31.7 0.8 %copy.9 = f32[1,128,1024]{2,1,0:T(8,128)} copy(f32[1,128,1024]{2,1,0:T(8,128)S(1)} %bitcast.8) | data formatting | bytes 1048576
